TPU v7x, 512 devices: a whole 4x8x8 slice. The times are simulated.
512 devices in a mesh: seq: 16 (over z, core), chan: 32 (over x, y).
Axes of the slice: x: 4, y: 8, z: 8, core: 2. Of those that a mesh axis runs over, the one named last changes fastest.
Arguments:
- tokens: bfloat16 [4096, 4096], P('seq', 'chan'), may hold values from -6 to 6
- w_in: bfloat16 [4096, 3, 4096], P(None, None, 'chan'), may hold values from -0.09375 to 0.09375
- filters: bfloat16 [256, 4096], P('chan'), may hold values from -0.09375 to 0.09375
- skip: float32 [4096], P('chan'), may hold values from 0.25 to 1.5
- w_out: bfloat16 [4096, 4096], P(None, 'chan'), may hold values from -0.09375 to 0.09375
Outputs:
- mixed: bfloat16 [4096, 4096], P('seq', 'chan')
All inputs are finite; a program needn't handle non-finite values.
Results may differ from a plain program's by a relative error of at most 0.015.
Values may be sent and summed in bfloat16 or wider, within the bound.
No kernel may reach another device: no remote copies, remote signals or barrier semaphores. Data moves between devices by JAX's collectives and lax.ppermute only.
A program may use at most 64 MiB of HBM per device.

v0:
```python
import math
import jax
import jax.numpy as jnp
from jax import lax
from jax.sharding import PartitionSpec as P


def toeplitz(padded, lead, offset, rows, cols):
    span = rows + cols
    segment = lax.dynamic_slice_in_dim(padded, lead + offset - cols + 1, span, 1)
    rolled = jnp.concatenate([segment[:, cols - 1 :], segment[:, : cols - 1]], axis=1)
    flat = jnp.tile(rolled, (1, cols))[:, : cols * (span - 1)]
    return flat.reshape(padded.shape[0], cols, span - 1)[:, :, :rows]


def apply_groups(matrix, values):
    groups = matrix.shape[0]
    grouped = values.reshape(values.shape[0], groups, -1)
    result = jnp.einsum("jgc,gji->gci", grouped, matrix, preferred_element_type=jnp.float32)
    return result.reshape(values.shape[1], matrix.shape[2]).T


def shards(tokens, w_in, filters, skip, w_out):
    block_len = tokens.shape[0]
    chans = w_out.shape[1]
    w_flat = w_in.reshape(w_in.shape[0], 3 * chans)
    rows = w_flat
    qkv = jnp.dot(
        lax.all_gather(tokens, "chan", axis=1, tiled=True), rows, preferred_element_type=jnp.float32
    )
    qkv = qkv.astype(jnp.bfloat16).reshape(block_len, 3, chans)
    query = qkv[:, 0]
    source = (qkv[:, 1].astype(jnp.float32) * qkv[:, 2].astype(jnp.float32)).astype(jnp.bfloat16)
    seq_rank = lax.axis_index("seq")
    lead = 2 * block_len
    row_first = seq_rank * block_len
    padded = jnp.pad(filters, ((0, 0), (lead, 1)))
    piece = lax.all_gather(source, "seq", axis=0, tiled=True)
    width = math.gcd(piece.shape[0], block_len)

    def visit(turn, carry):
        col_first = turn * width
        sub_block = lax.dynamic_slice_in_dim(piece, turn * width, width, 0)

        def contribute(acc):
            matrix = toeplitz(padded, lead, row_first - col_first, block_len, width)
            return acc + apply_groups(matrix, sub_block)

        return lax.cond(col_first < row_first + block_len, contribute, lambda acc: acc, carry)

    conv = lax.fori_loop(
        0, piece.shape[0] // width, visit, jnp.zeros((block_len, chans), jnp.float32)
    )
    gated = (
        query.astype(jnp.float32) * (conv + skip[None, :] * source.astype(jnp.float32))
    ).astype(jnp.bfloat16)
    rows = w_out
    mixed = jnp.dot(
        lax.all_gather(gated, "chan", axis=1, tiled=True), rows, preferred_element_type=jnp.float32
    )
    return mixed.astype(jnp.bfloat16)


def solution(mesh):
    in_specs = (
        P("seq", "chan"),
        P(None, None, "chan"),
        P("chan", None),
        P("chan"),
        P(None, "chan"),
    )
    out_specs = P("seq", "chan")
    return jax.shard_map(shards, mesh=mesh, in_specs=in_specs, out_specs=out_specs, check_vma=False)
```

profile of v0, /device:TPU:16, one launch (start us, length us, event | category | flops | bytes accessed | tf_op | source)
XLA Modules:
  0.0 409.9 jit_solution(13379084503499515155)
XLA Ops:
  6.5 0.0 copy-start
  6.5 0.0 all-gather.5.cloned.1.call-start
  6.5 0.7 all-gather.5.cloned.1.call-update
  7.3 0.0 all-gather.9.cloned.1.call-start
  7.3 4.7 %copy.9 = bf16[4096,3,128]{0,2,1:T(8,128)(2,1)} copy(bf16[4096,3,128]{2,0,1:T(8,128)(2,1)} %param.10) | data formatting | bytes 6291456 | tf_op args[1]
  12.0 82.4 %all-gather.5.cloned.1.call-done = bf16[256,4096]{1,0:T(8,128)(2,1)} async-done(((bf16[256,128]{1,0:T(8,128)(2,1)}), bf16[256,4096]{1,0:T(8,128)(2,1)}) %all-gather.5.cloned.1.call-update) | async-done | bytes 2097168 | tf_op jit(solution)/shard_map/all_gather | solution.py:29
  94.4 0.0 copy-start.1
  94.4 3.8 convolution_convert_fusion
  98.2 0.1 copy.10
  98.4 0.6 multiply_convert_fusion
  99.0 0.0 all-gather.9.cloned.1.call-update
  99.0 0.0 all-gather.7.cloned.1.call-start
  99.1 0.0 copy-done.1
  99.1 41.1 %all-gather.9.cloned.1.call-done = bf16[4096,1,128]{0,2,1:T(8,128)(2,1)} async-done(((bf16[256,1,128]{0,2,1:T(8,128)(2,1)}), bf16[4096,1,128]{0,2,1:T(8,128)(2,1)}) %all-gather.9.cloned.1.call-update) | async-done | bytes 1048592 | tf_op jit(solution)/shard_map/all_gather | solution.py:38
  140.2 0.0 copy-start.2
  140.2 11.8 %while.17 = (s32[]{:T(128)}, f32[256,128]{0,1:T(8,128)S(1)}, s32[]{:T(128)}, bf16[4096,128]{0,1:T(8,128)(2,1)}, s32[]{:T(128)}, /*index=5*/bf16[8,4609]{1,0:T(8,128)(2,1)S(1)}, s32[]{:T(128)}, s32[]{:T(128)}) while((s32[]{:T(128)}, f32[256,128]{0,1:T(8,128)S(1)}, s32[]{:T(128)}, bf16[4096,128]{0,1:T(8,128)(2,1)}, s32[]{:T(128)}, ...), condition=%wide.region_3.4_spmd, body=%wide.region_0.3_spmd.sunk | while | flops 16826380 | bytes 16466195 | solution.py:51
  140.3 11.2 %conditional.2 = (f32[256,128]{0,1:T(8,128)S(1)}) conditional(s32[]{:T(128)} %convert_element_type.67, f32[256,128]{0,1:T(8,128)S(1)} %get-tuple-element.249, (s32[]{:T(128)}, bf16[4096,128]{0,1:T(8,128)(2,1)}, s32[]{:T(128)}, bf16[8,4609]{1,0:T(8,128)(2,1)S(1)}, f32[256,128]{0,1:T(8,128)S(1)}) %tuple.50), branch_computations={%region_1.1_spmd, %region_2.2_spmd} | conditional | flops 16826376 | bytes 16466044 | solution.py:49
  140.3 0.1 constant_dynamic-slice_fusion
  140.4 0.1 constant_dynamic-slice_fusion.1
  140.5 0.1 pad_maximum_fusion
  140.5 0.1 tile.4
  140.7 0.1 slice.32
  140.8 4.4 %reshape.37 = bf16[1046528]{0:T(1024)(128)(2,1)} reshape(bf16[8,130816]{1,0:T(8,128)(2,1)S(1)} %slice.32) | data formatting | bytes 4186112 | tf_op jit(solution)/shard_map/while/body/eval_jaxpr/cond
  145.3 5.0 %reshape.28 = bf16[8,256,511]{2,1,0:T(8,128)(2,1)S(1)} reshape(bf16[1046528]{0:T(1024)(128)(2,1)} %reshape.37) | data formatting | bytes 4186112 | tf_op jit(solution)/shard_map/while/body/eval_jaxpr/cond/branch_1_fun/reshape | solution.py:13
  150.3 0.8 constant_dynamic-slice_fusion.2
  151.1 0.2 fusion
  152.1 0.0 copy-done.2
  152.1 0.7 fusion.4
  152.8 0.0 all-gather.7.cloned.1.call-update
  152.8 247.6 %all-gather.7.cloned.1.call-done = bf16[256,4096]{0,1:T(8,128)(2,1)} async-done(((bf16[256,128]{0,1:T(8,128)(2,1)}), bf16[256,4096]{0,1:T(8,128)(2,1)}) %all-gather.7.cloned.1.call-update) | async-done | bytes 2097168 | tf_op jit(solution)/shard_map/all_gather | solution.py:59
  400.4 0.0 copy-done
  400.4 3.0 convolution_convert_fusion.1
  (18 shorter events, 0.2 us)
Async XLA Ops:
  6.5 393.9 %copy-start = (bf16[4096,128]{1,0:T(8,128)(2,1)S(1)}, bf16[4096,128]{1,0:T(8,128)(2,1)}, u32[]{:S(2)}) copy-start(bf16[4096,128]{1,0:T(8,128)(2,1)} %param.13) | copy-start | bytes 3145732
  6.5 87.8 %all-gather.5.cloned.1.call-start = ((), (), s32[]{:S(2)}) async-start(), calls=%async_computation | async-start | bytes 2162688 | tf_op jit(solution)/shard_map/all_gather | solution.py:29
  7.3 133.0 %all-gather.9.cloned.1.call-start = ((), (), s32[]{:S(2)}) async-start(), calls=%async_computation.2 | async-start | bytes 1114112 | tf_op jit(solution)/shard_map/all_gather | solution.py:38
  94.4 4.7 %copy-start.1 = (bf16[8,4096]{1,0:T(8,128)(2,1)S(1)}, bf16[8,4096]{1,0:T(8,128)(2,1)}, u32[]{:S(2)}) copy-start(bf16[8,4096]{1,0:T(8,128)(2,1)} %param.11) | copy-start | bytes 196612
  99.0 301.4 %all-gather.7.cloned.1.call-start = ((), (), s32[]{:S(2)}) async-start(), calls=%async_computation.1 | async-start | bytes 2162688 | tf_op jit(solution)/shard_map/all_gather | solution.py:59
  140.2 11.8 %copy-start.2 = (f32[128]{0:T(128)S(1)}, f32[128]{0:T(128)}, u32[]{:S(2)}) copy-start(f32[128]{0:T(128)} %param.12) | copy-start | bytes 1540
Sparse Core Ops, SparseCore 0:
  10.4 83.9 all-gather.4
  99.1 41.0 all-gather.8
  152.9 247.4 all-gather.6
where the time goes:
time: 411 us; the launch traced here: 410 us
  waiting for transfers between devices  372 us (91%)
  local copies, waits for them, and re-layouts  15.6 us (4%)
  between operations  13.2 us (3%)
  matrix products  7.03 us (2%)
    all_gather x1, waiting for transfers between devices, shards(): lax.all_gather(gated, 'chan', axis=1, tiled=True)  248 us
    all_gather x1, waiting for transfers between devices, shards(): lax.all_gather(tokens, 'chan', axis=1, tiled=True)  82.4 us
    all_gather x1, waiting for transfers between devices, shards(): piece = lax.all_gather(source, 'seq', axis=0, tiled=True)  41.1 us
  transfers between devices with their start and end apart: 3, of which 3 were waited for; matrix products, arithmetic and copies ran while one was open for 1% of the time, Pallas kernels for 0%

commit v1 on v0

--- a/solution.py
+++ b/solution.py
@@ -56,7 +56,11 @@
     ).astype(jnp.bfloat16)
     rows = w_out
     mixed = jnp.dot(
-        lax.all_gather(gated, "chan", axis=1, tiled=True), rows, preferred_element_type=jnp.float32
+        jnp.concatenate(
+            lax.all_to_all(jnp.stack([gated] * lax.axis_size("chan")), "chan", 0, 0), axis=1
+        ),
+        rows,
+        preferred_element_type=jnp.float32,
     )
     return mixed.astype(jnp.bfloat16)
 

time: 411 us -> 373 us (0.908)
  the two profiles are of different devices: /device:TPU:16 before, /device:TPU:457 now
where the time goes in v1:
time: 373 us; the launch traced here: 372 us
  local copies, waits for them, and re-layouts  177 us (47%)
  waiting for transfers between devices  118 us (32%)
  blocking collectives  50.5 us (14%)
  between operations  13.5 us (4%)
  matrix products  9.1 us (2%)
    reshape x16, local copies, waits for them, and re-layouts, toeplitz(): return flat.reshape(padded.shape[0], cols, span - 1)[:, :, :rows]  80.1 us
    all_gather x1, waiting for transfers between devices, shards(): lax.all_gather(tokens, 'chan', axis=1, tiled=True)  74.1 us
    cond x16, local copies, waits for them, and re-layouts  71.3 us
    all_to_all x1, blocking collectives, shards(): lax.all_to_all(jnp.stack([gated] * lax.axis_size('chan')), 'chan', 0, 0)  50.5 us
    all_gather x1, waiting for transfers between devices, shards(): piece = lax.all_gather(source, 'seq', axis=0, tiled=True)  43.2 us
    dynamic_slice x16, local copies, waits for them, and re-layouts, visit(): sub_block = lax.dynamic_slice_in_dim(piece, turn * width, width, 0)  13.6 us
  transfers between devices with their start and end apart: 2, of which 2 were waited for; matrix products, arithmetic and copies ran while one was open for 1% of the time, Pallas kernels for 0%

profile of v1, /device:TPU:457, one launch (start us, length us, event | category | flops | bytes accessed | tf_op | source)
XLA Modules:
  0.0 372.2 jit_solution(7843591933172562167)
XLA Ops:
  12.0 74.1 %all-gather.4.cloned.1.call-done = bf16[256,4096]{1,0:T(8,128)(2,1)} async-done(((bf16[256,128]{1,0:T(8,128)(2,1)}), bf16[256,4096]{1,0:T(8,128)(2,1)}) %all-gather.4.cloned.1.call-update) | async-done | bytes 2097168 | tf_op jit(solution)/shard_map/all_gather | solution.py:29
  90.8 43.2 %all-gather.6.cloned.1.call-done = bf16[4096,1,128]{0,2,1:T(8,128)(2,1)} async-done(((bf16[256,1,128]{0,2,1:T(8,128)(2,1)}), bf16[4096,1,128]{0,2,1:T(8,128)(2,1)}) %all-gather.6.cloned.1.call-update) | async-done | bytes 1048592 | tf_op jit(solution)/shard_map/all_gather | solution.py:38
  134.1 179.0 %while.17 = (s32[]{:T(128)}, f32[256,128]{0,1:T(8,128)S(1)}, s32[]{:T(128)}, bf16[4096,128]{0,1:T(8,128)(2,1)}, s32[]{:T(128)}, /*index=5*/bf16[8,4609]{1,0:T(8,128)(2,1)S(1)}, s32[]{:T(128)}, s32[]{:T(128)}) while((s32[]{:T(128)}, f32[256,128]{0,1:T(8,128)S(1)}, s32[]{:T(128)}, bf16[4096,128]{0,1:T(8,128)(2,1)}, s32[]{:T(128)}, ...), condition=%wide.region_3.4_spmd, body=%wide.region_0.3_spmd.sunk | while | flops 16826380 | bytes 16466195 | solution.py:51
  134.1 11.2 %conditional.2 = (f32[256,128]{0,1:T(8,128)S(1)}) conditional(s32[]{:T(128)} %convert_element_type.67, f32[256,128]{0,1:T(8,128)S(1)} %get-tuple-element.249, (s32[]{:T(128)}, bf16[4096,128]{0,1:T(8,128)(2,1)}, s32[]{:T(128)}, bf16[8,4609]{1,0:T(8,128)(2,1)S(1)}, f32[256,128]{0,1:T(8,128)S(1)}) %tuple.50), branch_computations={%region_1.1_spmd, %region_2.2_spmd} | conditional | flops 16826376 | bytes 16466044 | solution.py:49
  139.1 5.0 %reshape.34 = bf16[8,256,511]{2,1,0:T(8,128)(2,1)S(1)} reshape(bf16[1046528]{0:T(1024)(128)(2,1)} %reshape.47) | data formatting | bytes 4186112 | tf_op jit(solution)/shard_map/while/body/eval_jaxpr/cond/branch_1_fun/reshape | solution.py:13
  145.3 11.2 %conditional.2 = (f32[256,128]{0,1:T(8,128)S(1)}) conditional(s32[]{:T(128)} %convert_element_type.67, f32[256,128]{0,1:T(8,128)S(1)} %get-tuple-element.249, (s32[]{:T(128)}, bf16[4096,128]{0,1:T(8,128)(2,1)}, s32[]{:T(128)}, bf16[8,4609]{1,0:T(8,128)(2,1)S(1)}, f32[256,128]{0,1:T(8,128)S(1)}) %tuple.50), branch_computations={%region_1.1_spmd, %region_2.2_spmd} | conditional | flops 16826376 | bytes 16466044 | solution.py:49
  150.3 5.0 %reshape.34 = bf16[8,256,511]{2,1,0:T(8,128)(2,1)S(1)} reshape(bf16[1046528]{0:T(1024)(128)(2,1)} %reshape.47) | data formatting | bytes 4186112 | tf_op jit(solution)/shard_map/while/body/eval_jaxpr/cond/branch_1_fun/reshape | solution.py:13
  156.5 11.2 %conditional.2 = (f32[256,128]{0,1:T(8,128)S(1)}) conditional(s32[]{:T(128)} %convert_element_type.67, f32[256,128]{0,1:T(8,128)S(1)} %get-tuple-element.249, (s32[]{:T(128)}, bf16[4096,128]{0,1:T(8,128)(2,1)}, s32[]{:T(128)}, bf16[8,4609]{1,0:T(8,128)(2,1)S(1)}, f32[256,128]{0,1:T(8,128)S(1)}) %tuple.50), branch_computations={%region_1.1_spmd, %region_2.2_spmd} | conditional | flops 16826376 | bytes 16466044 | solution.py:49
  161.5 5.0 %reshape.34 = bf16[8,256,511]{2,1,0:T(8,128)(2,1)S(1)} reshape(bf16[1046528]{0:T(1024)(128)(2,1)} %reshape.47) | data formatting | bytes 4186112 | tf_op jit(solution)/shard_map/while/body/eval_jaxpr/cond/branch_1_fun/reshape | solution.py:13
  167.6 11.2 %conditional.2 = (f32[256,128]{0,1:T(8,128)S(1)}) conditional(s32[]{:T(128)} %convert_element_type.67, f32[256,128]{0,1:T(8,128)S(1)} %get-tuple-element.249, (s32[]{:T(128)}, bf16[4096,128]{0,1:T(8,128)(2,1)}, s32[]{:T(128)}, bf16[8,4609]{1,0:T(8,128)(2,1)S(1)}, f32[256,128]{0,1:T(8,128)S(1)}) %tuple.50), branch_computations={%region_1.1_spmd, %region_2.2_spmd} | conditional | flops 16826376 | bytes 16466044 | solution.py:49
  172.7 5.0 %reshape.34 = bf16[8,256,511]{2,1,0:T(8,128)(2,1)S(1)} reshape(bf16[1046528]{0:T(1024)(128)(2,1)} %reshape.47) | data formatting | bytes 4186112 | tf_op jit(solution)/shard_map/while/body/eval_jaxpr/cond/branch_1_fun/reshape | solution.py:13
  178.8 11.2 %conditional.2 = (f32[256,128]{0,1:T(8,128)S(1)}) conditional(s32[]{:T(128)} %convert_element_type.67, f32[256,128]{0,1:T(8,128)S(1)} %get-tuple-element.249, (s32[]{:T(128)}, bf16[4096,128]{0,1:T(8,128)(2,1)}, s32[]{:T(128)}, bf16[8,4609]{1,0:T(8,128)(2,1)S(1)}, f32[256,128]{0,1:T(8,128)S(1)}) %tuple.50), branch_computations={%region_1.1_spmd, %region_2.2_spmd} | conditional | flops 16826376 | bytes 16466044 | solution.py:49
  183.8 5.0 %reshape.34 = bf16[8,256,511]{2,1,0:T(8,128)(2,1)S(1)} reshape(bf16[1046528]{0:T(1024)(128)(2,1)} %reshape.47) | data formatting | bytes 4186112 | tf_op jit(solution)/shard_map/while/body/eval_jaxpr/cond/branch_1_fun/reshape | solution.py:13
  190.0 11.2 %conditional.2 = (f32[256,128]{0,1:T(8,128)S(1)}) conditional(s32[]{:T(128)} %convert_element_type.67, f32[256,128]{0,1:T(8,128)S(1)} %get-tuple-element.249, (s32[]{:T(128)}, bf16[4096,128]{0,1:T(8,128)(2,1)}, s32[]{:T(128)}, bf16[8,4609]{1,0:T(8,128)(2,1)S(1)}, f32[256,128]{0,1:T(8,128)S(1)}) %tuple.50), branch_computations={%region_1.1_spmd, %region_2.2_spmd} | conditional | flops 16826376 | bytes 16466044 | solution.py:49
  195.0 5.0 %reshape.34 = bf16[8,256,511]{2,1,0:T(8,128)(2,1)S(1)} reshape(bf16[1046528]{0:T(1024)(128)(2,1)} %reshape.47) | data formatting | bytes 4186112 | tf_op jit(solution)/shard_map/while/body/eval_jaxpr/cond/branch_1_fun/reshape | solution.py:13
  201.2 11.2 %conditional.2 = (f32[256,128]{0,1:T(8,128)S(1)}) conditional(s32[]{:T(128)} %convert_element_type.67, f32[256,128]{0,1:T(8,128)S(1)} %get-tuple-element.249, (s32[]{:T(128)}, bf16[4096,128]{0,1:T(8,128)(2,1)}, s32[]{:T(128)}, bf16[8,4609]{1,0:T(8,128)(2,1)S(1)}, f32[256,128]{0,1:T(8,128)S(1)}) %tuple.50), branch_computations={%region_1.1_spmd, %region_2.2_spmd} | conditional | flops 16826376 | bytes 16466044 | solution.py:49
  206.2 5.0 %reshape.34 = bf16[8,256,511]{2,1,0:T(8,128)(2,1)S(1)} reshape(bf16[1046528]{0:T(1024)(128)(2,1)} %reshape.47) | data formatting | bytes 4186112 | tf_op jit(solution)/shard_map/while/body/eval_jaxpr/cond/branch_1_fun/reshape | solution.py:13
  212.4 11.2 %conditional.2 = (f32[256,128]{0,1:T(8,128)S(1)}) conditional(s32[]{:T(128)} %convert_element_type.67, f32[256,128]{0,1:T(8,128)S(1)} %get-tuple-element.249, (s32[]{:T(128)}, bf16[4096,128]{0,1:T(8,128)(2,1)}, s32[]{:T(128)}, bf16[8,4609]{1,0:T(8,128)(2,1)S(1)}, f32[256,128]{0,1:T(8,128)S(1)}) %tuple.50), branch_computations={%region_1.1_spmd, %region_2.2_spmd} | conditional | flops 16826376 | bytes 16466044 | solution.py:49
  217.4 5.0 %reshape.34 = bf16[8,256,511]{2,1,0:T(8,128)(2,1)S(1)} reshape(bf16[1046528]{0:T(1024)(128)(2,1)} %reshape.47) | data formatting | bytes 4186112 | tf_op jit(solution)/shard_map/while/body/eval_jaxpr/cond/branch_1_fun/reshape | solution.py:13
  223.6 11.2 %conditional.2 = (f32[256,128]{0,1:T(8,128)S(1)}) conditional(s32[]{:T(128)} %convert_element_type.67, f32[256,128]{0,1:T(8,128)S(1)} %get-tuple-element.249, (s32[]{:T(128)}, bf16[4096,128]{0,1:T(8,128)(2,1)}, s32[]{:T(128)}, bf16[8,4609]{1,0:T(8,128)(2,1)S(1)}, f32[256,128]{0,1:T(8,128)S(1)}) %tuple.50), branch_computations={%region_1.1_spmd, %region_2.2_spmd} | conditional | flops 16826376 | bytes 16466044 | solution.py:49
  228.6 5.0 %reshape.34 = bf16[8,256,511]{2,1,0:T(8,128)(2,1)S(1)} reshape(bf16[1046528]{0:T(1024)(128)(2,1)} %reshape.47) | data formatting | bytes 4186112 | tf_op jit(solution)/shard_map/while/body/eval_jaxpr/cond/branch_1_fun/reshape | solution.py:13
  234.8 11.2 %conditional.2 = (f32[256,128]{0,1:T(8,128)S(1)}) conditional(s32[]{:T(128)} %convert_element_type.67, f32[256,128]{0,1:T(8,128)S(1)} %get-tuple-element.249, (s32[]{:T(128)}, bf16[4096,128]{0,1:T(8,128)(2,1)}, s32[]{:T(128)}, bf16[8,4609]{1,0:T(8,128)(2,1)S(1)}, f32[256,128]{0,1:T(8,128)S(1)}) %tuple.50), branch_computations={%region_1.1_spmd, %region_2.2_spmd} | conditional | flops 16826376 | bytes 16466044 | solution.py:49
  239.8 5.0 %reshape.34 = bf16[8,256,511]{2,1,0:T(8,128)(2,1)S(1)} reshape(bf16[1046528]{0:T(1024)(128)(2,1)} %reshape.47) | data formatting | bytes 4186112 | tf_op jit(solution)/shard_map/while/body/eval_jaxpr/cond/branch_1_fun/reshape | solution.py:13
  246.0 11.2 %conditional.2 = (f32[256,128]{0,1:T(8,128)S(1)}) conditional(s32[]{:T(128)} %convert_element_type.67, f32[256,128]{0,1:T(8,128)S(1)} %get-tuple-element.249, (s32[]{:T(128)}, bf16[4096,128]{0,1:T(8,128)(2,1)}, s32[]{:T(128)}, bf16[8,4609]{1,0:T(8,128)(2,1)S(1)}, f32[256,128]{0,1:T(8,128)S(1)}) %tuple.50), branch_computations={%region_1.1_spmd, %region_2.2_spmd} | conditional | flops 16826376 | bytes 16466044 | solution.py:49
  251.0 5.0 %reshape.34 = bf16[8,256,511]{2,1,0:T(8,128)(2,1)S(1)} reshape(bf16[1046528]{0:T(1024)(128)(2,1)} %reshape.47) | data formatting | bytes 4186112 | tf_op jit(solution)/shard_map/while/body/eval_jaxpr/cond/branch_1_fun/reshape | solution.py:13
  257.2 11.2 %conditional.2 = (f32[256,128]{0,1:T(8,128)S(1)}) conditional(s32[]{:T(128)} %convert_element_type.67, f32[256,128]{0,1:T(8,128)S(1)} %get-tuple-element.249, (s32[]{:T(128)}, bf16[4096,128]{0,1:T(8,128)(2,1)}, s32[]{:T(128)}, bf16[8,4609]{1,0:T(8,128)(2,1)S(1)}, f32[256,128]{0,1:T(8,128)S(1)}) %tuple.50), branch_computations={%region_1.1_spmd, %region_2.2_spmd} | conditional | flops 16826376 | bytes 16466044 | solution.py:49
  262.2 5.0 %reshape.34 = bf16[8,256,511]{2,1,0:T(8,128)(2,1)S(1)} reshape(bf16[1046528]{0:T(1024)(128)(2,1)} %reshape.47) | data formatting | bytes 4186112 | tf_op jit(solution)/shard_map/while/body/eval_jaxpr/cond/branch_1_fun/reshape | solution.py:13
  268.4 11.2 %conditional.2 = (f32[256,128]{0,1:T(8,128)S(1)}) conditional(s32[]{:T(128)} %convert_element_type.67, f32[256,128]{0,1:T(8,128)S(1)} %get-tuple-element.249, (s32[]{:T(128)}, bf16[4096,128]{0,1:T(8,128)(2,1)}, s32[]{:T(128)}, bf16[8,4609]{1,0:T(8,128)(2,1)S(1)}, f32[256,128]{0,1:T(8,128)S(1)}) %tuple.50), branch_computations={%region_1.1_spmd, %region_2.2_spmd} | conditional | flops 16826376 | bytes 16466044 | solution.py:49
  279.5 11.2 %conditional.2 = (f32[256,128]{0,1:T(8,128)S(1)}) conditional(s32[]{:T(128)} %convert_element_type.67, f32[256,128]{0,1:T(8,128)S(1)} %get-tuple-element.249, (s32[]{:T(128)}, bf16[4096,128]{0,1:T(8,128)(2,1)}, s32[]{:T(128)}, bf16[8,4609]{1,0:T(8,128)(2,1)S(1)}, f32[256,128]{0,1:T(8,128)S(1)}) %tuple.50), branch_computations={%region_1.1_spmd, %region_2.2_spmd} | conditional | flops 16826376 | bytes 16466044 | solution.py:49
  290.7 11.2 %conditional.2 = (f32[256,128]{0,1:T(8,128)S(1)}) conditional(s32[]{:T(128)} %convert_element_type.67, f32[256,128]{0,1:T(8,128)S(1)} %get-tuple-element.249, (s32[]{:T(128)}, bf16[4096,128]{0,1:T(8,128)(2,1)}, s32[]{:T(128)}, bf16[8,4609]{1,0:T(8,128)(2,1)S(1)}, f32[256,128]{0,1:T(8,128)S(1)}) %tuple.50), branch_computations={%region_1.1_spmd, %region_2.2_spmd} | conditional | flops 16826376 | bytes 16466044 | solution.py:49
  301.9 11.2 %conditional.2 = (f32[256,128]{0,1:T(8,128)S(1)}) conditional(s32[]{:T(128)} %convert_element_type.67, f32[256,128]{0,1:T(8,128)S(1)} %get-tuple-element.249, (s32[]{:T(128)}, bf16[4096,128]{0,1:T(8,128)(2,1)}, s32[]{:T(128)}, bf16[8,4609]{1,0:T(8,128)(2,1)S(1)}, f32[256,128]{0,1:T(8,128)S(1)}) %tuple.50), branch_computations={%region_1.1_spmd, %region_2.2_spmd} | conditional | flops 16826376 | bytes 16466044 | solution.py:49
  313.4 50.5 %all_to_all.5 = bf16[32,256,128]{1,2,0:T(8,128)(2,1)S(1)} all-to-all(bf16[32,256,128]{1,2,0:T(8,128)(2,1)S(1)} %stack.2), channel_id=1, replica_groups=mesh['seq'=16,'chan'=32] {'chan'}, dimensions={0} | all-to-all | bytes 4194304 | tf_op jit(solution)/shard_map/all_to_all | solution.py:60
  (167 shorter events, 129.4 us)
Async XLA Ops:
  6.5 357.4 %copy-start = (bf16[4096,128]{1,0:T(8,128)(2,1)S(1)}, bf16[4096,128]{1,0:T(8,128)(2,1)}, u32[]{:S(2)}) copy-start(bf16[4096,128]{1,0:T(8,128)(2,1)} %param.13) | copy-start | bytes 3145732
  6.5 79.6 %all-gather.4.cloned.1.call-start = ((), (), s32[]{:S(2)}) async-start(), calls=%async_computation.1 | async-start | bytes 2162688 | tf_op jit(solution)/shard_map/all_gather | solution.py:29
  7.3 126.8 %all-gather.6.cloned.1.call-start = ((), (), s32[]{:S(2)}) async-start(), calls=%async_computation.2 | async-start | bytes 1114112 | tf_op jit(solution)/shard_map/all_gather | solution.py:38
  86.1 4.7 %copy-start.1 = (bf16[8,4096]{1,0:T(8,128)(2,1)S(1)}, bf16[8,4096]{1,0:T(8,128)(2,1)}, u32[]{:S(2)}) copy-start(bf16[8,4096]{1,0:T(8,128)(2,1)} %param.11) | copy-start | bytes 196612
  134.0 179.1 %copy-start.2 = (f32[128]{0:T(128)S(1)}, f32[128]{0:T(128)}, u32[]{:S(2)}) copy-start(f32[128]{0:T(128)} %param.12) | copy-start | bytes 1540
Sparse Core Ops, SparseCore 0:
  10.4 75.6 all-gather.3
  90.9 43.0 all-gather.5
